TPU v7x, 32 devices: a whole 2x2x4 slice. The times are simulated.
32 devices in a mesh: row: 4 (over z), col: 8 (over y, x, core).
Axes of the slice: x: 2, y: 2, z: 4, core: 2. Of those that a mesh axis runs over, the one named last changes fastest.
Arguments:
- embeddings: bfloat16 [4096, 768], P(('row', 'col')), may hold values from -4 to 4
- neg_ids: int32 [4, 2048], P('row', 'col'), may hold values from 0 to 16383, as said below
- neg_counts: int32 [4], P('row'), may hold values from 256 to 2048, as said below
- index_rows: bfloat16 [16384, 768], P('row'), may hold values from -4 to 4
Outputs:
- row_loss: float32 [4096], P(('row', 'col'))
- grad: float32 [4096, 768], P(('row', 'col'))
Inputs may be any that keep to these rules, and one draw needn't show every extreme that they name: `neg_counts`: every entry lies within the range; some lists are full (2048) and some hold exactly 256 entries. Index shard of an id is id // 4096. Among the 256 slots of one device (neg_ids[b, c * 256 : (c + 1) * 256]) at most 128 ids belong to any one index shard, and in every such run exactly 128 belong to one of them.
All inputs are finite; a program needn't handle non-finite values.
Results may differ from a plain program's by a relative error of at most 0.00059.
Values may be sent and summed in bfloat16 or wider, within the bound.
A program may use at most 128 MiB of HBM per device.

v0:
```python
import jax
import jax.numpy as jnp
from jax import lax
from jax.sharding import PartitionSpec as P

D = 768


def per_device(embeddings, neg_ids, neg_counts, index_rows):
    scale = D ** (-0.5)
    n_col = lax.axis_size("col")
    shard_rows = embeddings.shape[0]
    width = embeddings.shape[1]
    row_id = lax.axis_index("row")
    col_id = lax.axis_index("col")
    queries = lax.all_gather(embeddings, "col", axis=0, tiled=True)
    keys = lax.all_gather(embeddings, "row", axis=0, tiled=True)
    query_count = queries.shape[0]
    key_count = keys.shape[0]
    requests = lax.all_gather(neg_ids, "row", axis=0, tiled=True)
    owned_count = index_rows.shape[0]
    slot_count = neg_ids.shape[1]
    local_ids = requests - row_id * owned_count
    owned = (local_ids >= 0) & (local_ids < owned_count)
    picked = jnp.take(index_rows, jnp.clip(local_ids, 0, owned_count - 1), axis=0)
    picked = jnp.where(owned[..., None], picked, jnp.zeros_like(picked))
    fetched = lax.psum_scatter(
        picked.astype(jnp.float32).astype(jnp.bfloat16), "row", scatter_dimension=0, tiled=True
    ).astype(jnp.float32)
    negatives = fetched[0].astype(jnp.bfloat16)
    row_glob = row_id * query_count + jnp.arange(query_count, dtype=jnp.int32)
    key_local = jnp.arange(key_count, dtype=jnp.int32)
    col_glob = (key_local // shard_rows * n_col + col_id) * shard_rows + key_local % shard_rows
    scores = jnp.dot(queries, keys.T, preferred_element_type=jnp.float32) * scale
    scores = jnp.where(row_glob[:, None] == col_glob[None, :], -jnp.inf, scores)
    slot_glob = col_id * slot_count + jnp.arange(slot_count, dtype=jnp.int32)
    hard = jnp.dot(queries, negatives.T, preferred_element_type=jnp.float32) * scale
    hard = jnp.where((slot_glob < neg_counts[0])[None, :], hard, -jnp.inf)
    local_top = jnp.maximum(jnp.max(scores, axis=1), jnp.max(hard, axis=1))
    top = lax.pmax(local_top, "col")
    partial_value = jnp.sum(jnp.exp(scores - top[:, None]), axis=1) + jnp.sum(
        jnp.exp(hard - top[:, None]), axis=1
    )
    total = lax.psum(partial_value, "col")
    lse = top + jnp.log(total)
    own_f = embeddings.astype(jnp.float32)
    partner = own_f.reshape(shard_rows // 2, 2, width)[:, ::-1].reshape(shard_rows, width)
    positive = jnp.sum(own_f * partner, axis=1) * scale
    own_lse = lax.dynamic_slice_in_dim(lse, col_id * shard_rows, shard_rows, 0)
    row_loss = own_lse - positive
    target = (jnp.bitwise_xor(row_glob, 1)[:, None] == col_glob[None, :]).astype(jnp.float32)
    probs_grad = (jnp.exp(scores - lse[:, None]) - target).astype(jnp.bfloat16)
    hard_probs = jnp.exp(hard - lse[:, None]).astype(jnp.bfloat16)
    term = jnp.dot(probs_grad, keys, preferred_element_type=jnp.float32)
    query_part = lax.psum_scatter(
        term + jnp.dot(hard_probs, negatives, preferred_element_type=jnp.float32),
        "col",
        scatter_dimension=0,
        tiled=True,
    )
    key_part = lax.psum_scatter(
        lax.dot_general(
            probs_grad, queries, (((0,), (0,)), ((), ())), preferred_element_type=jnp.float32
        ),
        "row",
        scatter_dimension=0,
        tiled=True,
    )
    grad = query_part + key_part
    return (row_loss, grad)


def solution(mesh):
    return jax.shard_map(
        per_device,
        mesh=mesh,
        in_specs=(P(("row", "col"), None), P("row", "col"), P("row"), P("row", None)),
        out_specs=(P(("row", "col")), P(("row", "col"), None)),
        check_vma=False,
    )
```

profile of v0, /device:TPU:0, one launch (start us, length us, event | category | flops | bytes accessed | tf_op | source)
XLA Modules:
  0.0 196.2 jit_solution(175145558935563326)
XLA Ops:
  8.0 0.0 all-gather.3.cloned.1.call-start
  8.0 0.7 all-gather.3.cloned.1.call-update
  8.7 0.0 reduce-scatter.4.cloned.1.call-start
  8.8 12.8 %all-gather = s32[4,1,256]{2,1,0:T(1,128)S(1)} all-gather(s32[1,1,256]{2,1,0:T(1,128)} %bitcast.31), channel_id=1, replica_groups=mesh['row'=4,'col'=8] {'row'}, dimensions={0}, use_global_device_ids=true | all-gather | bytes 5120 | tf_op jit(solution)/shard_map/all_gather | solution.py:20
  21.7 8.1 %gather_fusion = bf16[1024,768]{1,0:T(8,128)(2,1)S(1)} fusion(bf16[4096,768]{1,0:T(8,128)(2,1)} %param.7, s32[1024]{0:T(1024)S(1)} %broadcast_clamp_fusion), kind=kCustom, calls=%fused_computation | custom fusion | bytes 3149824 | tf_op jit(solution)/shard_map/jit(_take)/gather | solution.py:25
  29.8 0.0 copy-start
  29.8 1.4 select_select_fusion
  31.2 0.0 reduce-scatter.4.cloned.1.call-update
  31.2 0.0 reduce-scatter.8.cloned.1.call-start
  32.0 0.0 copy-done
  32.0 26.3 %all_gather.10 = bf16[512,768]{1,0:T(8,128)(2,1)S(1)} all-gather(bf16[128,768]{1,0:T(8,128)(2,1)S(1)} %copy-done), channel_id=1, replica_groups=mesh['row'=4,'col'=8] {'row'}, dimensions={0}, use_global_device_ids=true | all-gather | bytes 983040 | tf_op jit(solution)/shard_map/all_gather | solution.py:17
  58.3 0.0 copy-start.1
  58.3 0.0 all-gather.3.cloned.1.call-done
  58.3 2.7 %fusion.18 = (f32[1024]{0:T(1024)S(1)}, f32[1024,512]{0,1:T(8,128)S(1)}) fusion(bf16[1024,768]{1,0:T(8,128)(2,1)} %all-gather.3.cloned.1.call-done, bf16[512,768]{1,0:T(8,128)(2,1)S(1)} %all_gather.10, s32[512]{0:T(512)S(1)} %fusion.12, s32[1024]{0:T(1024)S(1)} %iota_add_fusion), kind=kOutput, calls=%fused_computation.43 | convolution fusion | flops 807402496 | bytes 4466688 | tf_op jit(solution)/shard_map/dot_general | solution.py:34
  61.0 0.0 copy-done.1
  61.0 12.1 %reduce-scatter.4.cloned.1.call-done = bf16[1,256,768]{2,1,0:T(8,128)(2,1)} async-done(((bf16[4,256,768]{2,1,0:T(8,128)(2,1)}), bf16[1,256,768]{2,1,0:T(8,128)(2,1)}) %reduce-scatter.4.cloned.1.call-update) | async-done | bytes 393232 | tf_op jit(solution)/shard_map/reduce_scatter | solution.py:27
  73.1 2.2 %fusion.19 = (f32[1024]{0:T(1024)S(1)}, f32[256,1024]{1,0:T(8,128)S(1)}) fusion(bf16[1024,768]{1,0:T(8,128)(2,1)} %all-gather.3.cloned.1.call-done, bf16[1,256,768]{2,1,0:T(8,128)(2,1)} %reduce-scatter.4.cloned.1.call-done, pred[256]{0:T(512)(128)(4,1)S(1)} %add_compare_fusion), kind=kOutput, calls=%fused_computation.44 | convolution fusion | flops 403438592 | bytes 3019008 | tf_op jit(solution)/shard_map/dot_general | solution.py:37
  75.3 14.0 %pmax.7 = f32[1024]{0:T(1024)S(1)} all-reduce(f32[1024]{0:T(1024)S(1)} %max.9), channel_id=1, replica_groups=mesh['row'=4,'col'=8] {'col'}, use_global_device_ids=true, to_apply=%region_3.4 | all-reduce | flops 1024 | bytes 8192 | tf_op jit(solution)/shard_map/pmax | solution.py:40
  89.2 0.2 exponential_reduce_fusion.1
  89.4 0.3 exponential_reduce_fusion
  89.7 11.8 %psum.7 = f32[1024]{0:T(1024)S(1)} all-reduce(f32[1024]{0:T(1024)S(1)} %add.93), channel_id=1, replica_groups=mesh['row'=4,'col'=8] {'col'}, use_global_device_ids=true, to_apply=%region_6.7 | all-reduce | flops 1024 | bytes 8192 | tf_op jit(solution)/shard_map/psum | solution.py:44
  101.5 3.8 %fusion.16 = f32[512,768]{1,0:T(8,128)} fusion(bf16[1024,768]{1,0:T(8,128)(2,1)} %all-gather.3.cloned.1.call-done, f32[1024,512]{0,1:T(8,128)S(1)} %get-tuple-element.3, s32[1024]{0:T(1024)S(1)} %broadcast_xor_fusion, f32[1024]{0:T(1024)S(1)} %log_add_fusion, s32[512]{0:T(512)S(1)} %fusion.12), kind=kOutput, calls=%fused_computation.41 | convolution fusion | flops 807927808 | bytes 5253120 | tf_op jit(solution)/shard_map/dot_general | solution.py:62
  105.3 0.0 reduce-scatter.8.cloned.1.call-update
  105.3 0.0 reduce-scatter.6.cloned.1.call-start
  105.4 0.0 copy-start.2
  105.4 2.3 %fusion.17 = f32[1024,768]{1,0:T(8,128)S(1)} fusion(bf16[512,768]{1,0:T(8,128)(2,1)} %copy-done.1, f32[1024,512]{0,1:T(8,128)S(1)} %get-tuple-element.3, s32[1024]{0:T(1024)S(1)} %broadcast_xor_fusion, f32[1024]{0:T(1024)S(1)} %log_add_fusion, s32[512]{0:T(512)S(1)} %fusion.12), kind=kOutput, calls=%fused_computation.42 | convolution fusion | flops 807927808 | bytes 6039552 | tf_op jit(solution)/shard_map/dot_general | solution.py:54
  107.7 0.0 copy-done.2
  107.7 2.3 %convolution_add_fusion = f32[1024,768]{1,0:T(8,128)} fusion(f32[1024,768]{1,0:T(8,128)S(1)} %fusion.17, f32[256,1024]{1,0:T(8,128)S(1)} %get-tuple-element.5, f32[1024]{0:T(1024)S(1)} %log_add_fusion, bf16[1,256,768]{2,1,0:T(8,128)(2,1)S(1)} %copy-done.2), kind=kOutput, calls=%fused_computation.4 | convolution fusion | flops 403963904 | bytes 7737344 | tf_op jit(solution)/shard_map/dot_general | solution.py:56
  110.0 0.0 reduce-scatter.6.cloned.1.call-update
  110.0 0.2 reshape.55
  110.2 1.1 rev.3
  111.4 0.3 reshape.56
  111.6 0.1 multiply_reduce_fusion
  111.8 0.6 multiply_subtract_fusion
  112.3 26.1 %reduce-scatter.8.cloned.1.call-done = f32[128,768]{1,0:T(8,128)} async-done(((f32[512,768]{1,0:T(8,128)}), f32[128,768]{1,0:T(8,128)}) %reduce-scatter.8.cloned.1.call-update) | async-done | bytes 393232 | tf_op jit(solution)/shard_map/reduce_scatter | solution.py:61
  138.4 48.2 %reduce-scatter.6.cloned.1.call-done = f32[128,768]{1,0:T(8,128)} async-done(((f32[1024,768]{1,0:T(8,128)}), f32[128,768]{1,0:T(8,128)}) %reduce-scatter.6.cloned.1.call-update) | async-done | bytes 393232 | tf_op jit(solution)/shard_map/reduce_scatter | solution.py:55
  186.7 1.9 add.97
  (14 shorter events, 0.1 us)
Async XLA Ops:
  8.0 50.3 %all-gather.3.cloned.1.call-start = ((), (), s32[]{:S(2)}) async-start(), calls=%async_computation.3 | async-start | bytes 1769472 | tf_op jit(solution)/shard_map/all_gather | solution.py:16
  8.7 64.4 %reduce-scatter.4.cloned.1.call-start = ((), (), s32[]{:S(2)}) async-start(), calls=%async_computation.4 | async-start | bytes 1966080 | tf_op jit(solution)/shard_map/reduce_scatter | solution.py:27
  29.8 2.2 %copy-start = (bf16[128,768]{1,0:T(8,128)(2,1)S(1)}, bf16[128,768]{1,0:T(8,128)(2,1)}, u32[]{:S(2)}) copy-start(bf16[128,768]{1,0:T(8,128)(2,1)} %param.4) | copy-start | bytes 589828
  31.2 107.2 %reduce-scatter.8.cloned.1.call-start = ((), (), s32[]{:S(2)}) async-start(), calls=%async_computation.6 | async-start | bytes 1966080 | tf_op jit(solution)/shard_map/reduce_scatter | solution.py:61
  58.3 2.7 %copy-start.1 = (bf16[512,768]{1,0:T(8,128)(2,1)}, bf16[512,768]{1,0:T(8,128)(2,1)S(1)}, u32[]{:S(2)}) copy-start(bf16[512,768]{1,0:T(8,128)(2,1)S(1)} %all_gather.10) | copy-start | bytes 2359300
  105.3 81.4 %reduce-scatter.6.cloned.1.call-start = ((), (), s32[]{:S(2)}) async-start(), calls=%async_computation.5 | async-start | bytes 3538944 | tf_op jit(solution)/shard_map/reduce_scatter | solution.py:55
  105.4 2.3 %copy-start.2 = (bf16[1,256,768]{2,1,0:T(8,128)(2,1)S(1)}, bf16[1,256,768]{2,1,0:T(8,128)(2,1)}, u32[]{:S(2)}) copy-start(bf16[1,256,768]{2,1,0:T(8,128)(2,1)} %reduce-scatter.4.cloned.1.call-done) | copy-start | bytes 1179652
Sparse Core Ops, SparseCore 0:
  10.7 28.4 all-gather.2
Sparse Core Ops, SparseCore 1:
  31.3 41.7 reduce-scatter.3
  105.4 33.0 reduce-scatter.7
  141.7 44.9 reduce-scatter.5
where the time goes:
time: 197 us; the launch traced here: 196 us
  waiting for transfers between devices  87.1 us (44%)
  blocking collectives  64.9 us (33%)
  between operations  16.5 us (8%)
  matrix products  13.3 us (7%)
  local copies, waits for them, and re-layouts  9.65 us (5%)
  other arithmetic  4.59 us (2%)
    reduce_scatter x1, waiting for transfers between devices, per_device(): lax.psum_scatter(term + jnp.dot(hard_probs, negatives, preferred_element_...  48.2 us
    all_gather x1, blocking collectives, per_device(): keys = lax.all_gather(embeddings, 'row', axis=0, tiled=True)  26.3 us
    reduce_scatter x1, waiting for transfers between devices, per_device(): lax.psum_scatter(lax.dot_general(probs_grad, queries, (((0,), (0,)), ((),...  26.1 us
    pmax x1, blocking collectives, per_device(): top = lax.pmax(local_top, 'col')  14 us
    all_gather x1, blocking collectives, per_device(): requests = lax.all_gather(neg_ids, 'row', axis=0, tiled=True)  12.8 us
    reduce_scatter x1, waiting for transfers between devices, per_device(): lax.psum_scatter(picked.astype(jnp.float32).astype(jnp.bfloat16), 'row',...  12.1 us
    psum x1, blocking collectives, per_device(): total = lax.psum(partial_value, 'col')  11.8 us
    gather x1, local copies, waits for them, and re-layouts, per_device(): jnp.take(index_rows, jnp.clip(local_ids, 0, owned_count - 1), axis=0)  8.07 us
  transfers between devices with their start and end apart: 4, of which 3 were waited for; matrix products, arithmetic and copies ran while one was open for 10% of the time, Pallas kernels for 0%

commit v1 on v0

v1 whole, which is shorter than its diff:
```python
import functools

import jax
import jax.numpy as jnp
from jax import lax
from jax.experimental import pallas as pl
from jax.experimental.pallas import tpu as pltpu
from jax.sharding import PartitionSpec as P

D = 768
F32 = jnp.float32
BF16 = jnp.bfloat16
NT = (((1,), (1,)), ((), ()))
TN = (((0,), (0,)), ((), ()))


def kernel(n_row, n_col, cap, emb, ids, cnt, index, loss, grad,
           q, kn, s, sel, cid_s, cid_r, idx_v, hot, ng_s, ng_r, st_s, st_r, lk_s, lk_r,
           sib_s, sib_r, keep, red_s, red_r,
           idx_sem, cid_ss, cid_rs, k_ss, k_rs, q_ss, q_rs, ng_ss, ng_rs, st_ss, st_rs,
           lk_ss, lk_rs, sib_ss, sib_rs, red_ss, red_rs):
    scale = D ** (-0.5)
    n_chip = n_col // 2
    rows = emb.shape[0]
    slots = ids.shape[1]
    owned = index.shape[0]
    n_key = n_row * rows
    r = lax.axis_index("row")
    c = lax.axis_index("col")
    chip = c // 2
    core = c % 2

    def row_peer(e):
        return (lax.rem(r + e, n_row), c)

    def col_peer(m, b):
        other = core if b == 0 else 1 - core
        return (r, lax.rem(chip + m, n_chip) * 2 + other)

    def remote(src, dst, send_sem, recv_sem, device):
        return pltpu.make_async_remote_copy(
            src_ref=src, dst_ref=dst, send_sem=send_sem, recv_sem=recv_sem,
            device_id=device, device_id_type=pl.DeviceIdType.MESH)

    col_steps = [(m, b) for m in range(n_chip) for b in range(2) if m or b]

    def mirror(m, b):
        return 2 * ((n_chip - m) % n_chip) + b

    load = pltpu.make_async_copy(index, idx_v, idx_sem)
    load.start()
    barrier = pltpu.get_barrier_semaphore()
    for e in range(1, n_row):
        pl.semaphore_signal(barrier, inc=1, device_id=row_peer(e),
                            device_id_type=pl.DeviceIdType.MESH)
    for m, b in col_steps:
        pl.semaphore_signal(barrier, inc=1, device_id=col_peer(m, b),
                            device_id_type=pl.DeviceIdType.MESH)

    listed = ids[...]
    masks, locals_ = [], []
    for e in range(n_row):
        local = listed - lax.rem(r + e, n_row) * owned
        masks.append(jnp.where((local >= 0) & (local < owned), 1.0, 0.0).astype(F32))
        locals_.append(local)
    before = (lax.broadcasted_iota(jnp.int32, (slots, slots), 0)
              < lax.broadcasted_iota(jnp.int32, (slots, slots), 1))
    mask = jnp.concatenate(masks, axis=0)
    rank = jnp.dot(mask.astype(BF16), jnp.where(before, 1.0, 0.0).astype(BF16),
                   preferred_element_type=F32)
    place = lax.broadcasted_iota(jnp.int32, (128, slots), 0).astype(F32)
    line = lax.broadcasted_iota(jnp.int32, (8, slots), 0)
    for e in range(n_row):
        chosen = jnp.where((place == rank[e:e + 1, :]) & (masks[e] > 0.5), 1.0, 0.0)
        sel[e * cap:(e + 1) * cap, :] = chosen[:cap].astype(BF16)
        local = jnp.where(masks[e] > 0.5, locals_[e], 0)
        high = jnp.right_shift(local, 6).astype(F32)
        low = jnp.bitwise_and(local, 63).astype(F32)
        parts = jnp.where(line == 0, high, jnp.where(line == 1, low, 1.0))
        got = lax.dot_general(parts.astype(BF16), chosen.astype(BF16), NT,
                              preferred_element_type=F32)
        packed = jnp.where(got[2:3] > 0.5, got[0:1] * 64.0 + got[1:2], -1.0)
        wide = jnp.broadcast_to(packed, (8, 128))
        if e == 0:
            cid_r[0] = wide
        else:
            cid_s[e] = wide

    pl.semaphore_wait(barrier, n_row - 1 + len(col_steps))
    cid_copies, k_copies, q_copies = {}, {}, {}
    for e in range(1, n_row):
        back = n_row - e
        cid_copies[e] = remote(cid_s.at[e], cid_r.at[back], cid_ss.at[e], cid_rs.at[back],
                               row_peer(e))
        cid_copies[e].start()
    for e in range(1, n_row):
        back = n_row - e
        k_copies[e] = remote(emb, kn.at[pl.ds(back * rows, rows)], k_ss.at[e], k_rs.at[back],
                             row_peer(e))
        k_copies[e].start()
    own_rows = pl.ds(pl.multiple_of(core * rows, rows), rows)
    for m, b in col_steps:
        q_copies[m, b] = remote(emb, q.at[chip, own_rows], q_ss.at[2 * m + b],
                                q_rs.at[mirror(m, b)], col_peer(m, b))
        q_copies[m, b].start()
    kn[0:rows, :] = emb[...]
    q[chip, own_rows, :] = emb[...]

    columns = []
    for e in range(n_row):
        if e:
            remote(cid_s.at[e], cid_r.at[e], cid_ss.at[e], cid_rs.at[e], row_peer(e)).wait_recv()
        columns.append(jnp.broadcast_to(cid_r[e][0:1, :], (128, 128)).T[:cap])
    wanted = jnp.concatenate(columns, axis=0)
    lane = lax.broadcasted_iota(jnp.int32, (n_row * cap, 128), 1).astype(F32)
    for j in range(owned // 128):
        hot[:, j * 128:(j + 1) * 128] = jnp.where(
            wanted == lane + float(j * 128), 1.0, 0.0).astype(BF16)
    load.wait()
    for j in range(D // 256):
        part = pl.ds(j * 256, 256)
        picked = jnp.dot(hot[...], idx_v[:, part], preferred_element_type=F32).astype(BF16)
        ng_r[0:cap, part] = picked[:cap]
        ng_s[:, part] = picked
    ng_copies = {}
    for e in range(1, n_row):
        back = n_row - e
        ng_copies[e] = remote(ng_s.at[pl.ds(e * cap, cap)], ng_r.at[pl.ds(back * cap, cap)],
                              ng_ss.at[e], ng_rs.at[back], row_peer(e))
        ng_copies[e].start()

    for e in range(1, n_row):
        remote(emb, kn.at[pl.ds(e * rows, rows)], k_ss.at[e], k_rs.at[e], row_peer(e)).wait_recv()
    own = lax.broadcasted_iota(jnp.int32, (rows, 2 * rows), 0)
    other = lax.broadcasted_iota(jnp.int32, (rows, 2 * rows), 1) - core * rows
    same = own == other
    partner = jnp.bitwise_xor(own, 1) == other
    positive = None
    for m in range(n_chip):
        at = lax.rem(chip + m, n_chip)
        for b in range(2):
            if m or b:
                remote(emb, q.at[at, pl.ds(pl.multiple_of((core if b == 0 else 1 - core) * rows, rows), rows)],
                       q_ss.at[2 * m + b], q_rs.at[2 * m + b], col_peer(m, b)).wait_recv()
        block = lax.dot_general(kn[0:n_key, :], q[at], NT, preferred_element_type=F32) * scale
        if m == 0:
            first = block[0:rows]
            positive = jnp.sum(jnp.where(partner, first, 0.0), axis=0, keepdims=True)
            s[at, 0:rows, :] = jnp.where(same, -jnp.inf, first)
            s[at, rows:n_key, :] = block[rows:]
        else:
            s[at, 0:n_key, :] = block

    for e in range(1, n_row):
        remote(ng_s.at[pl.ds(e * cap, cap)], ng_r.at[pl.ds(e * cap, cap)], ng_ss.at[e],
               ng_rs.at[e], row_peer(e)).wait_recv()
    kn[n_key:n_key + slots, :] = lax.dot_general(
        sel[...], ng_r[...], TN, preferred_element_type=F32).astype(BF16)
    live = (lax.broadcasted_iota(jnp.int32, (slots, 2 * rows), 0) + c * slots) < cnt[0]
    for m in range(n_chip):
        at = lax.rem(chip + m, n_chip)
        hard = lax.dot_general(kn[n_key:n_key + slots, :], q[at], NT,
                               preferred_element_type=F32) * scale
        hard = jnp.where(live, hard, -jnp.inf)
        s[at, n_key:n_key + slots, :] = hard
        block = s[at, 0:n_key, :]
        top = jnp.maximum(jnp.max(block, axis=0, keepdims=True),
                          jnp.max(hard, axis=0, keepdims=True))
        total = (jnp.sum(jnp.exp(block - top), axis=0, keepdims=True)
                 + jnp.sum(jnp.exp(hard - top), axis=0, keepdims=True))
        st_s[at, 0:1, :] = top
        st_s[at, 1:2, :] = total
    st_copies = {}
    for m, b in col_steps:
        st_copies[m, b] = remote(st_s, st_r.at[mirror(m, b)], st_ss.at[2 * m + b],
                                 st_rs.at[mirror(m, b)], col_peer(m, b))
        st_copies[m, b].start()
    for m, b in col_steps:
        remote(st_s, st_r.at[2 * m + b], st_ss.at[2 * m + b], st_rs.at[2 * m + b],
               col_peer(m, b)).wait_recv()

    def lse_of(at):
        tops = [st_s[at, 0:1, :]] + [st_r[2 * m + b, at, 0:1, :] for m, b in col_steps]
        sums = [st_s[at, 1:2, :]] + [st_r[2 * m + b, at, 1:2, :] for m, b in col_steps]
        top = functools.reduce(jnp.maximum, tops)
        return top + jnp.log(sum(v * jnp.exp(t - top) for t, v in zip(tops, sums)))

    own_lse = lse_of(chip)
    both = jnp.concatenate([own_lse, own_lse - positive], axis=0)
    half = jnp.where(core == 0, both[:, 0:rows], both[:, rows:2 * rows])
    loss[...] = half[1:2]
    mine = jnp.broadcast_to(half[0:1], (8, rows))
    lk_s[...] = mine
    lk_copies = {}
    for e in range(1, n_row):
        back = n_row - e
        lk_copies[e] = remote(lk_s, lk_r.at[back], lk_ss.at[e], lk_rs.at[back], row_peer(e))
        lk_copies[e].start()
    key_lse = [jnp.broadcast_to(half[0:1], (rows, rows)).T]
    for e in range(1, n_row):
        remote(lk_s, lk_r.at[e], lk_ss.at[e], lk_rs.at[e], row_peer(e)).wait_recv()
        key_lse.append(jnp.broadcast_to(lk_r[e][0:1, :], (rows, rows)).T)
    key_lse = jnp.concatenate(key_lse, axis=0)
    key_lse = jnp.concatenate([key_lse, key_lse], axis=1)

    sib_copies, red_copies = {}, {}
    sibling = col_peer(0, 1)

    def pass_on(m):
        sib_copies[m].wait_recv()
        red_s[m] = keep[m] + sib_r[m]
        back = n_chip - m
        red_copies[m] = remote(red_s.at[m], red_r.at[back], red_ss.at[m], red_rs.at[back],
                               col_peer(m, 0))
        red_copies[m].start()

    order = list(range(1, n_chip)) + [0]
    for n, m in enumerate(order):
        at = lax.rem(chip + m, n_chip)
        lse = own_lse if m == 0 else lse_of(at)
        as_query = jnp.exp(s[at] - lse)
        as_key = jnp.exp(s[at, 0:n_key, :] - key_lse)
        if m == 0:
            target = jnp.where(partner, 1.0, 0.0)
            as_query = jnp.concatenate([as_query[0:rows] - target, as_query[rows:]], axis=0)
            as_key = jnp.concatenate([as_key[0:rows] - target, as_key[rows:]], axis=0)
        term = lax.dot_general(as_query.astype(BF16), kn[...], TN, preferred_element_type=F32)
        term += lax.dot_general(as_key.astype(BF16), kn[0:n_key, :], TN,
                                preferred_element_type=F32)
        keep[m] = jnp.where(core == 0, term[0:rows], term[rows:])
        sib_s[m] = jnp.where(core == 0, term[rows:], term[0:rows])
        sib_copies[m] = remote(sib_s.at[m], sib_r.at[m], sib_ss.at[m], sib_rs.at[m], sibling)
        sib_copies[m].start()
        if n >= 1:
            pass_on(order[n - 1])
    sib_copies[0].wait_recv()
    total = keep[0] + sib_r[0]
    for m in range(1, n_chip):
        remote(red_s.at[m], red_r.at[m], red_ss.at[m], red_rs.at[m], col_peer(m, 0)).wait_recv()
        total += red_r[m]
    grad[...] = total

    for copies in (cid_copies, k_copies, q_copies, ng_copies, st_copies, lk_copies,
                   sib_copies, red_copies):
        for copy in copies.values():
            copy.wait_send()


def per_device(n_row, n_col, embeddings, neg_ids, neg_counts, index_rows):
    rows = embeddings.shape[0]
    slots = neg_ids.shape[1]
    owned = index_rows.shape[0]
    cap = 2 * slots // n_row
    n_chip = n_col // 2
    n_key = n_row * rows
    vmem = pltpu.VMEM
    dma = pltpu.SemaphoreType.DMA
    loss, grad = pl.pallas_call(
        functools.partial(kernel, n_row, n_col, cap),
        out_shape=(jax.ShapeDtypeStruct((1, rows), F32),
                   jax.ShapeDtypeStruct((rows, D), F32)),
        in_specs=[pl.BlockSpec(memory_space=vmem), pl.BlockSpec(memory_space=vmem),
                  pl.BlockSpec(memory_space=pltpu.SMEM), pl.BlockSpec(memory_space=pl.ANY)],
        out_specs=(pl.BlockSpec(memory_space=vmem), pl.BlockSpec(memory_space=vmem)),
        scratch_shapes=[
            vmem((n_chip, 2 * rows, D), BF16),
            vmem((n_key + slots, D), BF16),
            vmem((n_chip, n_key + slots, 2 * rows), F32),
            vmem((n_row * cap, slots), BF16),
            vmem((n_row, 8, 128), F32),
            vmem((n_row, 8, 128), F32),
            vmem((owned, D), BF16),
            vmem((n_row * cap, owned), BF16),
            vmem((n_row * cap, D), BF16),
            vmem((n_row * cap, D), BF16),
            vmem((n_chip, 2, 2 * rows), F32),
            vmem((n_col, n_chip, 2, 2 * rows), F32),
            vmem((8, rows), F32),
            vmem((n_row, 8, rows), F32),
            vmem((n_chip, rows, D), F32),
            vmem((n_chip, rows, D), F32),
            vmem((n_chip, rows, D), F32),
            vmem((n_chip, rows, D), F32),
            vmem((n_chip, rows, D), F32),
            dma,
            dma((n_row,)), dma((n_row,)), dma((n_row,)), dma((n_row,)),
            dma((n_col,)), dma((n_col,)), dma((n_row,)), dma((n_row,)),
            dma((n_col,)), dma((n_col,)), dma((n_row,)), dma((n_row,)),
            dma((n_chip,)), dma((n_chip,)), dma((n_chip,)), dma((n_chip,)),
        ],
        compiler_params=pltpu.CompilerParams(
            collective_id=0, has_side_effects=True, vmem_limit_bytes=58 * 1024 * 1024),
    )(embeddings, neg_ids, neg_counts, index_rows)
    return loss.reshape(rows), grad


def solution(mesh):
    return jax.shard_map(
        functools.partial(per_device, mesh.shape["row"], mesh.shape["col"]),
        mesh=mesh,
        in_specs=(P(("row", "col"), None), P("row", "col"), P("row"), P("row", None)),
        out_specs=(P(("row", "col")), P(("row", "col"), None)),
        check_vma=False,
    )
```

time: 197 us -> 77.9 us (0.40)
  waiting for transfers between devices: 87.1 us -> 0 us
  Pallas kernels: 0 us -> 73.5 us
  blocking collectives: 64.9 us -> 0 us
  between operations: 16.5 us -> 1.28 us
  matrix products: 13.3 us -> 0 us
  local copies, waits for them, and re-layouts: 9.65 us -> 2.89 us
  other arithmetic: 4.59 us -> 0 us
    reduce_scatter x3 -> x0, waiting for transfers between devices: 86.4 us -> none  [the longest x1 48.2 us: per_device(): lax.psum_scatter(term + jnp.dot(hard_probs, negatives, preferred_element_...]
    pallas_call x0 -> x1, Pallas kernels: none -> 73.5 us  [per_device(): pl.pallas_call(functools.partial(kernel, n_row, n_col, cap), out_shape=(j...]
    all_gather x2 -> x0, blocking collectives: 39.1 us -> none  [the longest x1 26.3 us: per_device(): keys = lax.all_gather(embeddings, 'row', axis=0, tiled=True)]
    pmax x1 -> x0, blocking collectives: 14 us -> none  [per_device(): top = lax.pmax(local_top, 'col')]
    dot_general x5 -> x0, matrix products: 13.3 us -> none  [the longest x1 3.75 us: per_device(): lax.dot_general(probs_grad, queries, (((0,), (0,)), ((), ())), preferred_...]
    psum x1 -> x0, blocking collectives: 11.8 us -> none  [per_device(): total = lax.psum(partial_value, 'col')]
    gather x1 -> x0, local copies, waits for them, and re-layouts: 8.07 us -> none  [per_device(): jnp.take(index_rows, jnp.clip(local_ids, 0, owned_count - 1), axis=0)]
    unnamed x8 -> x2, local copies, waits for them, and re-layouts: 0.02 us -> 2.89 us
  transfers between devices with their start and end apart: 4 -> 0, of which waited for: 3 -> 0; matrix products, arithmetic and copies ran while one was open for 10% -> 0% of each run, Pallas kernels for 0% -> 0%
where the time goes in v1:
time: 77.9 us; the launch traced here: 77.7 us
  Pallas kernels  73.5 us (94%)
  local copies, waits for them, and re-layouts  2.89 us (4%)
  between operations  1.28 us (2%)
    pallas_call x1, Pallas kernels, per_device(): pl.pallas_call(functools.partial(kernel, n_row, n_col, cap), out_shape=(j...  73.5 us
    unnamed x2, local copies, waits for them, and re-layouts  2.89 us

profile of v1, /device:TPU:0, one launch (start us, length us, event | category | flops | bytes accessed | tf_op | source)
XLA Modules:
  0.0 77.7 jit_solution(4039827712198346144)
XLA Ops:
  1.3 73.5 %shard_map.59 = (f32[1,128]{1,0:T(1,128)}, f32[128,768]{1,0:T(8,128)}) custom-call(bf16[128,768]{1,0:T(8,128)(2,1)} %emb.1, s32[1,256]{1,0:T(1,128)} %ids.1, s32[1]{0:T(128)S(6)} %copy.8.cnt, bf16[4096,768]{1,0:T(8,128)(2,1)} %index.1), custom_call_target="tpu_custom_call" | custom-call | tf_op jit(solution)/shard_map/pallas_call | solution.py:258
  74.8 1.1 %copy.9 = f32[128]{0:T(128)} copy(f32[128]{0:T(128)} %bitcast.1) | data formatting | bytes 1024
  75.9 1.8 %copy.10 = f32[128,768]{1,0:T(8,128)} copy(f32[128,768]{1,0:T(8,128)} %get-tuple-element.9) | data formatting | bytes 786432

commit v2 on v1

--- a/solution.py
+++ b/solution.py
@@ -16,9 +16,9 @@
 
 def kernel(n_row, n_col, cap, emb, ids, cnt, index, loss, grad,
            q, kn, s, sel, cid_s, cid_r, idx_v, hot, ng_s, ng_r, st_s, st_r, lk_s, lk_r,
-           sib_s, sib_r, keep, red_s, red_r,
+           sib_s, sib_r, keep, red_s, red_r, unit_s, unit_r, acc,
            idx_sem, cid_ss, cid_rs, k_ss, k_rs, q_ss, q_rs, ng_ss, ng_rs, st_ss, st_rs,
-           lk_ss, lk_rs, sib_ss, sib_rs, red_ss, red_rs):
+           lk_ss, lk_rs, sib_ss, sib_rs, red_ss, red_rs, unit_ss, unit_rs):
     scale = D ** (-0.5)
     n_chip = n_col // 2
     rows = emb.shape[0]
@@ -87,23 +87,52 @@
             cid_s[e] = wide
 
     pl.semaphore_wait(barrier, n_row - 1 + len(col_steps))
-    cid_copies, k_copies, q_copies = {}, {}, {}
+    cid_copies, q_copies = {}, {}
+
+    def key_slot(owner):
+        return kn.at[pl.ds(pl.multiple_of(owner * rows, rows), rows)]
+
+    def key_copy(way, h):
+        step = 1 if way == 0 else -1
+        owner = r - step * (h - 1)
+        src = emb if h == 1 else key_slot(owner)
+        return remote(src, key_slot(owner), k_ss.at[way, h], k_rs.at[way, h], (r + step, c))
+
+    def sends(way, h):
+        return (r + 1 < n_row) & (r >= h - 1) if way == 0 else (r >= 1) & (r + h - 1 < n_row)
+
+    def key_send(h):
+        for way in range(2):
+            @pl.when(sends(way, h))
+            def _():
+                key_copy(way, h).start()
+
+    def key_sent(h):
+        for way in range(2):
+            @pl.when(sends(way, h))
+            def _():
+                key_copy(way, h).wait_send()
+
+    def key_wait(h):
+        for way in range(2):
+            @pl.when((r >= h) if way == 0 else (r + h < n_row))
+            def _():
+                owner = r - h if way == 0 else r + h
+                remote(emb, key_slot(owner), k_ss.at[way, h], k_rs.at[way, h],
+                       row_peer(1)).wait_recv()
+
     for e in range(1, n_row):
         back = n_row - e
         cid_copies[e] = remote(cid_s.at[e], cid_r.at[back], cid_ss.at[e], cid_rs.at[back],
                                row_peer(e))
         cid_copies[e].start()
-    for e in range(1, n_row):
-        back = n_row - e
-        k_copies[e] = remote(emb, kn.at[pl.ds(back * rows, rows)], k_ss.at[e], k_rs.at[back],
-                             row_peer(e))
-        k_copies[e].start()
+    key_send(1)
     own_rows = pl.ds(pl.multiple_of(core * rows, rows), rows)
     for m, b in col_steps:
         q_copies[m, b] = remote(emb, q.at[chip, own_rows], q_ss.at[2 * m + b],
                                 q_rs.at[mirror(m, b)], col_peer(m, b))
         q_copies[m, b].start()
-    kn[0:rows, :] = emb[...]
+    kn[pl.ds(pl.multiple_of(r * rows, rows), rows), :] = emb[...]
     q[chip, own_rows, :] = emb[...]
 
     columns = []
@@ -122,6 +151,9 @@
         picked = jnp.dot(hot[...], idx_v[:, part], preferred_element_type=F32).astype(BF16)
         ng_r[0:cap, part] = picked[:cap]
         ng_s[:, part] = picked
+    if n_row > 2:
+        key_wait(1)
+        key_send(2)
     ng_copies = {}
     for e in range(1, n_row):
         back = n_row - e
@@ -129,10 +161,13 @@
                               ng_ss.at[e], ng_rs.at[back], row_peer(e))
         ng_copies[e].start()
 
-    for e in range(1, n_row):
-        remote(emb, kn.at[pl.ds(e * rows, rows)], k_ss.at[e], k_rs.at[e], row_peer(e)).wait_recv()
-    own = lax.broadcasted_iota(jnp.int32, (rows, 2 * rows), 0)
-    other = lax.broadcasted_iota(jnp.int32, (rows, 2 * rows), 1) - core * rows
+    for h in range(2, n_row - 1):
+        key_wait(h)
+        key_send(h + 1)
+    key_wait(n_row - 1)
+    own = lax.broadcasted_iota(jnp.int32, (n_key, 2 * rows), 0) - r * rows
+    other = lax.broadcasted_iota(jnp.int32, (n_key, 2 * rows), 1) - core * rows
+    other = jnp.where((other >= 0) & (other < rows), other, 2 * n_key)
     same = own == other
     partner = jnp.bitwise_xor(own, 1) == other
     positive = None
@@ -144,12 +179,9 @@
                        q_ss.at[2 * m + b], q_rs.at[2 * m + b], col_peer(m, b)).wait_recv()
         block = lax.dot_general(kn[0:n_key, :], q[at], NT, preferred_element_type=F32) * scale
         if m == 0:
-            first = block[0:rows]
-            positive = jnp.sum(jnp.where(partner, first, 0.0), axis=0, keepdims=True)
-            s[at, 0:rows, :] = jnp.where(same, -jnp.inf, first)
-            s[at, rows:n_key, :] = block[rows:]
-        else:
-            s[at, 0:n_key, :] = block
+            positive = jnp.sum(jnp.where(partner, block, 0.0), axis=0, keepdims=True)
+            block = jnp.where(same, -jnp.inf, block)
+        s[at, 0:n_key, :] = block
 
     for e in range(1, n_row):
         remote(ng_s.at[pl.ds(e * cap, cap)], ng_r.at[pl.ds(e * cap, cap)], ng_ss.at[e],
@@ -191,42 +223,61 @@
     loss[...] = half[1:2]
     mine = jnp.broadcast_to(half[0:1], (8, rows))
     lk_s[...] = mine
+    lk_r[r] = mine
     lk_copies = {}
     for e in range(1, n_row):
-        back = n_row - e
-        lk_copies[e] = remote(lk_s, lk_r.at[back], lk_ss.at[e], lk_rs.at[back], row_peer(e))
+        lk_copies[e] = remote(lk_s, lk_r.at[r], lk_ss.at[e], lk_rs.at[n_row - e], row_peer(e))
         lk_copies[e].start()
-    key_lse = [jnp.broadcast_to(half[0:1], (rows, rows)).T]
-    for e in range(1, n_row):
-        remote(lk_s, lk_r.at[e], lk_ss.at[e], lk_rs.at[e], row_peer(e)).wait_recv()
+
+    def query_term(m):
+        at = lax.rem(chip + m, n_chip)
+        weight = jnp.exp(s[at] - (own_lse if m == 0 else lse_of(at)))
+        if m == 0:
+            weight = jnp.concatenate(
+                [weight[0:n_key] - jnp.where(partner, 1.0, 0.0), weight[n_key:]], axis=0)
+        return lax.dot_general(weight.astype(BF16), kn[...], TN, preferred_element_type=F32)
+
+    def key_term(m):
+        weight = jnp.exp(s[lax.rem(chip + m, n_chip), 0:n_key, :] - key_lse)
+        if m == 0:
+            weight = weight - jnp.where(partner, 1.0, 0.0)
+        return lax.dot_general(weight.astype(BF16), kn[0:n_key, :], TN,
+                               preferred_element_type=F32)
+
+    order = list(range(1, n_chip)) + [0]
+    early = order[:2]
+    for n, m in enumerate(early):
+        acc[n] = query_term(m)
+    key_lse = []
+    for e in range(1, n_row):
+        remote(lk_s, lk_r.at[lax.rem(r + e, n_row)], lk_ss.at[e], lk_rs.at[e],
+               row_peer(e)).wait_recv()
+    for e in range(n_row):
         key_lse.append(jnp.broadcast_to(lk_r[e][0:1, :], (rows, rows)).T)
     key_lse = jnp.concatenate(key_lse, axis=0)
     key_lse = jnp.concatenate([key_lse, key_lse], axis=1)
 
-    sib_copies, red_copies = {}, {}
+    sib_copies, red_copies, unit_copies = {}, {}, {}
     sibling = col_peer(0, 1)
 
     def pass_on(m):
         sib_copies[m].wait_recv()
-        red_s[m] = keep[m] + sib_r[m]
+        both_sum = keep[m] + sib_r[m]
+        largest = jnp.maximum(jnp.max(jnp.abs(both_sum), axis=1, keepdims=True), 1e-30)
+        unit = largest * (1.0 / 32000.0)
+        steps = jnp.round(both_sum * (1.0 / unit))
+        red_s[m] = steps.astype(jnp.int32).astype(jnp.int16)
+        unit_s[m] = jnp.broadcast_to(unit, (rows, 128)).T[0:8]
         back = n_chip - m
         red_copies[m] = remote(red_s.at[m], red_r.at[back], red_ss.at[m], red_rs.at[back],
                                col_peer(m, 0))
         red_copies[m].start()
-
-    order = list(range(1, n_chip)) + [0]
+        unit_copies[m] = remote(unit_s.at[m], unit_r.at[back], unit_ss.at[m], unit_rs.at[back],
+                                col_peer(m, 0))
+        unit_copies[m].start()
+
     for n, m in enumerate(order):
-        at = lax.rem(chip + m, n_chip)
-        lse = own_lse if m == 0 else lse_of(at)
-        as_query = jnp.exp(s[at] - lse)
-        as_key = jnp.exp(s[at, 0:n_key, :] - key_lse)
-        if m == 0:
-            target = jnp.where(partner, 1.0, 0.0)
-            as_query = jnp.concatenate([as_query[0:rows] - target, as_query[rows:]], axis=0)
-            as_key = jnp.concatenate([as_key[0:rows] - target, as_key[rows:]], axis=0)
-        term = lax.dot_general(as_query.astype(BF16), kn[...], TN, preferred_element_type=F32)
-        term += lax.dot_general(as_key.astype(BF16), kn[0:n_key, :], TN,
-                                preferred_element_type=F32)
+        term = acc[n] + key_term(m) if m in early else query_term(m) + key_term(m)
         keep[m] = jnp.where(core == 0, term[0:rows], term[rows:])
         sib_s[m] = jnp.where(core == 0, term[rows:], term[0:rows])
         sib_copies[m] = remote(sib_s.at[m], sib_r.at[m], sib_ss.at[m], sib_rs.at[m], sibling)
@@ -237,11 +288,16 @@
     total = keep[0] + sib_r[0]
     for m in range(1, n_chip):
         remote(red_s.at[m], red_r.at[m], red_ss.at[m], red_rs.at[m], col_peer(m, 0)).wait_recv()
-        total += red_r[m]
+        remote(unit_s.at[m], unit_r.at[m], unit_ss.at[m], unit_rs.at[m],
+               col_peer(m, 0)).wait_recv()
+        unit = jnp.broadcast_to(unit_r[m][0:1, :], (128, rows)).T[:, 0:1]
+        total += red_r[m].astype(jnp.int32).astype(F32) * unit
     grad[...] = total
 
-    for copies in (cid_copies, k_copies, q_copies, ng_copies, st_copies, lk_copies,
-                   sib_copies, red_copies):
+    for h in range(1, n_row):
+        key_sent(h)
+    for copies in (cid_copies, q_copies, ng_copies, st_copies, lk_copies,
+                   sib_copies, red_copies, unit_copies):
         for copy in copies.values():
             copy.wait_send()
 
@@ -280,13 +336,17 @@
             vmem((n_chip, rows, D), F32),
             vmem((n_chip, rows, D), F32),
             vmem((n_chip, rows, D), F32),
-            vmem((n_chip, rows, D), F32),
-            vmem((n_chip, rows, D), F32),
+            vmem((n_chip, rows, D), jnp.int16),
+            vmem((n_chip, rows, D), jnp.int16),
+            vmem((n_chip, 8, rows), F32),
+            vmem((n_chip, 8, rows), F32),
+            vmem((2, 2 * rows, D), F32),
             dma,
-            dma((n_row,)), dma((n_row,)), dma((n_row,)), dma((n_row,)),
+            dma((n_row,)), dma((n_row,)), dma((2, n_row)), dma((2, n_row)),
             dma((n_col,)), dma((n_col,)), dma((n_row,)), dma((n_row,)),
             dma((n_col,)), dma((n_col,)), dma((n_row,)), dma((n_row,)),
             dma((n_chip,)), dma((n_chip,)), dma((n_chip,)), dma((n_chip,)),
+            dma((n_chip,)), dma((n_chip,)),
         ],
         compiler_params=pltpu.CompilerParams(
             collective_id=0, has_side_effects=True, vmem_limit_bytes=58 * 1024 * 1024),

time: 77.9 us -> 70 us (0.90)
  Pallas kernels: 73.5 us -> 65.6 us
    pallas_call x1, Pallas kernels: 73.5 us -> 65.6 us  [per_device(): pl.pallas_call(functools.partial(kernel, n_row, n_col, cap), out_shape=(j...]
where the time goes in v2:
time: 70 us; the launch traced here: 69.8 us
  Pallas kernels  65.6 us (94%)
  local copies, waits for them, and re-layouts  2.89 us (4%)
  between operations  1.28 us (2%)
    pallas_call x1, Pallas kernels, per_device(): pl.pallas_call(functools.partial(kernel, n_row, n_col, cap), out_shape=(j...  65.6 us
    unnamed x2, local copies, waits for them, and re-layouts  2.89 us

profile of v2, /device:TPU:0, one launch (start us, length us, event | category | flops | bytes accessed | tf_op | source)
XLA Modules:
  0.0 69.8 jit_solution(1670169940553739665)
XLA Ops:
  1.3 65.6 %shard_map.59 = (f32[1,128]{1,0:T(1,128)}, f32[128,768]{1,0:T(8,128)}) custom-call(bf16[128,768]{1,0:T(8,128)(2,1)} %emb.1, s32[1,256]{1,0:T(1,128)} %ids.1, s32[1]{0:T(128)S(6)} %copy.8.cnt, bf16[4096,768]{1,0:T(8,128)(2,1)} %index.1), custom_call_target="tpu_custom_call" | custom-call | tf_op jit(solution)/shard_map/pallas_call | solution.py:314
  66.9 1.1 %copy.9 = f32[128]{0:T(128)} copy(f32[128]{0:T(128)} %bitcast.1) | data formatting | bytes 1024
  68.0 1.8 %copy.10 = f32[128,768]{1,0:T(8,128)} copy(f32[128,768]{1,0:T(8,128)} %get-tuple-element.9) | data formatting | bytes 786432

commit v3 on v2

--- a/solution.py
+++ b/solution.py
@@ -164,24 +164,44 @@
     for h in range(2, n_row - 1):
         key_wait(h)
         key_send(h + 1)
-    key_wait(n_row - 1)
+    for m, b in col_steps:
+        at = lax.rem(chip + m, n_chip)
+        half = pl.multiple_of((core if b == 0 else 1 - core) * rows, rows)
+        remote(emb, q.at[at, pl.ds(half, rows)], q_ss.at[2 * m + b], q_rs.at[2 * m + b],
+               col_peer(m, b)).wait_recv()
+
+    def score(owner):
+        part = pl.ds(pl.multiple_of(owner * rows, rows), rows)
+        for m in range(n_chip):
+            at = lax.rem(chip + m, n_chip)
+            s[at, part, :] = lax.dot_general(kn[part, :], q[at], NT,
+                                             preferred_element_type=F32) * scale
+
+    def score_away(h):
+        @pl.when(r >= h)
+        def _():
+            score(r - h)
+
+        @pl.when(r + h < n_row)
+        def _():
+            score(r + h)
+
+    score(r)
+    own = lax.broadcasted_iota(jnp.int32, (rows, 2 * rows), 0)
+    other = lax.broadcasted_iota(jnp.int32, (rows, 2 * rows), 1) - core * rows
+    own_part = pl.ds(pl.multiple_of(r * rows, rows), rows)
+    block = s[chip, own_part, :]
+    positive = jnp.sum(jnp.where(jnp.bitwise_xor(own, 1) == other, block, 0.0), axis=0,
+                       keepdims=True)
+    s[chip, own_part, :] = jnp.where(own == other, -jnp.inf, block)
+    for h in range(1, n_row):
+        if h == n_row - 1:
+            key_wait(h)
+        score_away(h)
     own = lax.broadcasted_iota(jnp.int32, (n_key, 2 * rows), 0) - r * rows
     other = lax.broadcasted_iota(jnp.int32, (n_key, 2 * rows), 1) - core * rows
     other = jnp.where((other >= 0) & (other < rows), other, 2 * n_key)
-    same = own == other
     partner = jnp.bitwise_xor(own, 1) == other
-    positive = None
-    for m in range(n_chip):
-        at = lax.rem(chip + m, n_chip)
-        for b in range(2):
-            if m or b:
-                remote(emb, q.at[at, pl.ds(pl.multiple_of((core if b == 0 else 1 - core) * rows, rows), rows)],
-                       q_ss.at[2 * m + b], q_rs.at[2 * m + b], col_peer(m, b)).wait_recv()
-        block = lax.dot_general(kn[0:n_key, :], q[at], NT, preferred_element_type=F32) * scale
-        if m == 0:
-            positive = jnp.sum(jnp.where(partner, block, 0.0), axis=0, keepdims=True)
-            block = jnp.where(same, -jnp.inf, block)
-        s[at, 0:n_key, :] = block
 
     for e in range(1, n_row):
         remote(ng_s.at[pl.ds(e * cap, cap)], ng_r.at[pl.ds(e * cap, cap)], ng_ss.at[e],

time: 70 us -> 67.6 us (0.966)
  Pallas kernels: 65.6 us -> 63.2 us
    pallas_call x1, Pallas kernels: 65.6 us -> 63.2 us  [per_device(): pl.pallas_call(functools.partial(kernel, n_row, n_col, cap), out_shape=(j...]
where the time goes in v3:
time: 67.6 us; the launch traced here: 67.4 us
  Pallas kernels  63.2 us (93%)
  local copies, waits for them, and re-layouts  2.89 us (4%)
  between operations  1.28 us (2%)
    pallas_call x1, Pallas kernels, per_device(): pl.pallas_call(functools.partial(kernel, n_row, n_col, cap), out_shape=(j...  63.2 us
    unnamed x2, local copies, waits for them, and re-layouts  2.89 us

profile of v3, /device:TPU:0, one launch (start us, length us, event | category | flops | bytes accessed | tf_op | source)
XLA Modules:
  0.0 67.4 jit_solution(4635469121402919119)
XLA Ops:
  1.3 63.2 %shard_map.59 = (f32[1,128]{1,0:T(1,128)}, f32[128,768]{1,0:T(8,128)}) custom-call(bf16[128,768]{1,0:T(8,128)(2,1)} %emb.1, s32[1,256]{1,0:T(1,128)} %ids.1, s32[1]{0:T(128)S(6)} %copy.8.cnt, bf16[4096,768]{1,0:T(8,128)(2,1)} %index.1), custom_call_target="tpu_custom_call" | custom-call | tf_op jit(solution)/shard_map/pallas_call | solution.py:334
  64.5 1.1 %copy.9 = f32[128]{0:T(128)} copy(f32[128]{0:T(128)} %bitcast.1) | data formatting | bytes 1024
  65.6 1.8 %copy.10 = f32[128,768]{1,0:T(8,128)} copy(f32[128,768]{1,0:T(8,128)} %get-tuple-element.9) | data formatting | bytes 786432
